TPU v7x, 128 devices: a whole 4x4x4 slice. The times are simulated.
128 devices in a mesh: comp: 4 (over x), cell: 32 (over y, z, core).
Axes of the slice: x: 4, y: 4, z: 4, core: 2. Of those that a mesh axis runs over, the one named last changes fastest.
Arguments:
- biomass: float32 [48, 64, 16384], P(None, None, ('comp', 'cell')), may hold values from 0.1 to 2
- patch_area: float32 [48, 16384], P(None, ('comp', 'cell')), may hold values from 0.005 to 0.04
- cohort_traits: float32 [4, 64], replicated, may hold values from 0.1 to 1
- cell_forcing: float32 [5, 16384], P(None, ('comp', 'cell')), may hold values from 0.1 to 1
- disturb_weight: float32 [4, 16384], P(None, ('comp', 'cell')), may hold values from 0 to 0.25
- transitions: float32 [4, 48, 48], replicated, may hold values from 0 to 1
- land_source: int32 [131072], P(('comp', 'cell')), may hold values from -1 to 127, as said below
- pair_share: float32 [131072], P(('comp', 'cell')), may hold values from 0.05 to 0.35
- river_target: int32 [131072], P(('comp', 'cell')), may hold values from -1 to 2047, as said below
- downstream_step: int32 [262144], P(('comp', 'cell')), may hold values from 0 to 2047
- river_water: float32 [4, 262144], P(None, ('comp', 'cell')), may hold values from 0.5 to 2
- river_rates: float32 [4, 262144], P(None, ('comp', 'cell')), may hold values from 0.05 to 0.8
- capacity: float32 [262144], P(('comp', 'cell')), may hold values from 0.5 to 5
Outputs:
- new_biomass: float32 [48, 64, 16384], P(None, None, ('comp', 'cell'))
- flooded: float32 [16384], P(('comp', 'cell'))
- river_state: float32 [4, 262144], P(None, ('comp', 'cell'))
Inputs may be any that keep to these rules, and one draw needn't show every extreme that they name: `land_source`: A device's list has one block of 8 rows for each receiving device, in comp+cell order; live rows come first in every block, padding rows hold -1. Every device has at least one full block, and one receiving device gets full blocks from every device. `river_target`: row s of block i on device j is live exactly when row s of block j on device i of land_source is live, and then names the receiving river cell of device j; padding rows hold -1.
All inputs are finite; a program needn't handle non-finite values.
Results may differ from a plain program's by a relative error of at most 0.0001.
Values sent between devices are 32-bit elements; how exact they have to be, the bound alone decides.
A program may use at most 64 MiB of HBM per device.

v0:
```python
import jax
import jax.numpy as jnp
from jax import lax
from jax.sharding import PartitionSpec as P

NSUB = 12
highest = lax.Precision.HIGHEST


def in_blocks(value, dim, devices):
    before, after = (value.shape[:dim], value.shape[dim + 1 :])
    return jnp.moveaxis(value.reshape(*before, devices, -1, *after), dim, 0)


def in_order(blocks, dim):
    blocks = jnp.moveaxis(blocks, 0, dim)
    lengths = blocks.shape
    return blocks.reshape(*lengths[:dim], lengths[dim] * lengths[dim + 1], *lengths[dim + 2 :])


def joined_exchange(value, axis, axes, splits, concats):
    sizes = [lax.axis_size(a) for a in axes]
    blocks = in_blocks(value, splits[0], sizes[0])
    blocks = jnp.moveaxis(in_blocks(blocks, splits[1] + 1, sizes[1]), 0, 1)
    inside = blocks.shape[2:]
    blocks = blocks.reshape(-1, *inside)
    blocks = lax.all_to_all(blocks, axis, split_axis=0, concat_axis=0, tiled=True)
    blocks = in_order(blocks.reshape(*sizes, *inside), concats[0] + 1)
    return in_order(blocks, concats[1])


def from_behind(value, axis, steps):
    count = lax.axis_size(axis)
    initial, last = (max(0, -steps), min(count, count - steps))
    return lax.ppermute(value, axis, [(source, source + steps) for source in range(initial, last)])


def canopy(biomass, patch_area, cohort_traits, cell_forcing):
    leaf_area = biomass * cohort_traits[0][None, :, None]
    bin_count = biomass.shape[1]
    taller_mask = (jnp.arange(bin_count)[None, :] > jnp.arange(bin_count)[:, None]).astype(
        jnp.float32
    )
    leaf_above = jnp.einsum("kj,pjc->pkc", taller_mask, leaf_area, precision=highest)
    light_level = cell_forcing[0]
    assimilation = (
        cohort_traits[1][None, :, None]
        * leaf_area
        * jnp.exp(-0.05 * leaf_above)
        * (light_level / (light_level + 0.5))[None, None, :]
    )
    transpiration = 0.5 * jnp.sum(patch_area * jnp.sum(assimilation, axis=1), axis=0)
    wet_rain = cell_forcing[1] * cell_forcing[2]
    runoff = jnp.stack(
        [
            wet_rain * (1.0 - cell_forcing[4]),
            wet_rain * cell_forcing[4],
            cell_forcing[3] * jnp.exp(-0.5 * transpiration),
        ]
    )
    grown_mass = biomass * (1.0 - 0.1 * cohort_traits[2])[None, :, None] + 0.5 * assimilation
    return (grown_mass, runoff)


def transit(grown_mass, disturb_weight, transitions):
    patches, bin_count, cell_count = grown_mass.shape
    flat_mass = grown_mass.reshape(patches, bin_count * cell_count)
    transited = jnp.zeros_like(grown_mass)
    for kind_index in range(transitions.shape[0]):
        moved_mass = jnp.dot(
            transitions[kind_index],
            flat_mass,
            precision=highest,
            preferred_element_type=jnp.float32,
        )
        transited = (
            transited
            + moved_mass.reshape(patches, bin_count, cell_count)
            * disturb_weight[kind_index][None, None, :]
        )
    return transited


def scatter_pair(outflow, slots, segments):
    return jax.ops.segment_sum(outflow.T, slots, num_segments=segments).T


def shards(
    biomass,
    patch_area,
    cohort_traits,
    cell_forcing,
    disturb_weight,
    transitions,
    land_source,
    pair_share,
    river_target,
    downstream_step,
    river_water,
    river_rates,
    capacity,
):
    land_cells = biomass.shape[2]
    rivers = river_water.shape[1]
    comp_parts = lax.axis_size("comp")
    grown_mass, runoff = canopy(biomass, patch_area, cohort_traits, cell_forcing)
    is_live = land_source >= 0
    safe_source = jnp.where(is_live, land_source, 0)
    pair_values = jnp.where(
        is_live[None, :], pair_share[None, :] * jnp.take(runoff, safe_source, axis=1), 0.0
    )
    arrived = joined_exchange(
        pair_values.reshape(3, comp_parts, -1), ("comp", "cell"), ("comp", "cell"), (1, 2), (1, 2)
    ).reshape(3, -1)
    transited = transit(grown_mass, disturb_weight, transitions)
    has_target = river_target >= 0
    safe_target = jnp.where(has_target, river_target, rivers)
    runoff_in = jax.ops.segment_sum(arrived.T, safe_target, num_segments=rivers + 1)[:rivers].T
    local_cell = jnp.arange(rivers, dtype=jnp.int32)
    down_slot = jnp.where(downstream_step > 0, local_cell + downstream_step, 2 * rivers)
    fraction = 1.0 / NSUB
    surface_in = fraction * runoff_in[0:2]
    deep_in = jnp.stack([fraction * runoff_in[2], jnp.zeros_like(runoff_in[2])])
    hill_rate = river_rates[0:2]
    channel_rate = river_rates[2:4]

    def substep(sub_index, state_pair):
        hill_water, channel = state_pair
        hill_out = hill_rate * hill_water
        outflow = channel_rate * channel
        spread = scatter_pair(outflow, down_slot, 2 * rivers + 1)
        from_above = from_behind(spread[:, rivers : 2 * rivers], ("comp", "cell"), 1)
        inflow = spread[:, :rivers] + from_above
        return (hill_water - hill_out + surface_in, channel - outflow + hill_out + inflow + deep_in)

    hill_water, channel = lax.fori_loop(0, NSUB, substep, (river_water[0:2], river_water[2:4]))
    stored_total = channel[0] + channel[1]
    inundation = stored_total / (stored_total + capacity)
    flood_back = jnp.where(has_target, inundation[jnp.where(has_target, river_target, 0)], 0.0)
    returned = lax.all_to_all(
        lax.all_to_all(
            flood_back.reshape(comp_parts, -1), "cell", split_axis=1, concat_axis=1, tiled=True
        ),
        "comp",
        split_axis=0,
        concat_axis=0,
        tiled=True,
    ).reshape(-1)
    flooded = jax.ops.segment_sum(
        pair_share * returned,
        jnp.where(is_live, land_source, land_cells),
        num_segments=land_cells + 1,
    )[:land_cells]
    new_biomass = transited * jnp.exp(-cohort_traits[3][None, :, None] * flooded[None, None, :])
    river_state = jnp.concatenate([hill_water, channel], axis=0)
    return (new_biomass, flooded, river_state)


def solution(mesh):
    return jax.shard_map(
        shards,
        mesh=mesh,
        in_specs=(
            P(None, None, ("comp", "cell")),
            P(None, ("comp", "cell")),
            P(),
            P(None, ("comp", "cell")),
            P(None, ("comp", "cell")),
            P(),
            P(("comp", "cell")),
            P(("comp", "cell")),
            P(("comp", "cell")),
            P(("comp", "cell")),
            P(None, ("comp", "cell")),
            P(None, ("comp", "cell")),
            P(("comp", "cell")),
        ),
        out_specs=(P(None, None, ("comp", "cell")), P(("comp", "cell")), P(None, ("comp", "cell"))),
        check_vma=False,
    )
```

profile of v0, /device:TPU:8, one launch (start us, length us, event | category | flops | bytes accessed | tf_op | source)
XLA Modules:
  0.0 398.8 jit_solution(263364392975987532)
XLA Ops:
  3.6 3.6 fusion.52
  7.4 2.8 gather_fusion
  12.3 10.5 %all-to-all-start = ((f32[128,3,1,8]{3,2,1,0:T(1,128)}), f32[128,3,1,8]{3,2,1,0:T(1,128)S(1)}, u32[]{:S(2)}, u32[]{:S(2)}) async-start(f32[128,3,1,8]{3,2,1,0:T(1,128)} %bitcast.27), calls=%async_computation | async-start | bytes 393216 | tf_op jit(solution)/shard_map/all_to_all | solution.py:27
  22.8 3.7 fusion.18
  26.5 3.6 fusion.21
  30.3 3.7 fusion.24
  39.1 6.5 %scatter_custom_fusion.1 = f32[2049,3]{1,0:T(8,128)S(1)} fusion(s32[1024]{0:T(1024)S(1)} %get-tuple-element.76, f32[1024,3]{1,0:T(8,128)S(1)} %copy.88, f32[]{:T(128)} %constant.23.clone.1), kind=kCustom, calls=%fused_computation.45 | custom fusion | flops 3072 | bytes 24592 | tf_op jit(solution)/shard_map/scatter-add | solution.py:118
  48.2 300.2 %while.12 = (s32[]{:T(128)}, f32[2,2048]{0,1:T(8,128)}, f32[2,2048]{0,1:T(8,128)S(1)}, f32[2,2048]{0,1:T(8,128)}, f32[2,2048]{0,1:T(8,128)}, /*index=5*/f32[2,20...) while((s32[]{:T(128)}, f32[2,2048]{0,1:T(8,128)}, f32[2,2048]{0,1:T(8,128)S(1)}, ...), condition=%wide.region_5.6_spmd, body=%wide.region_3.5_spmd.sunk | while | flops 45058 | bytes 1851629 | solution.py:136
  48.2 12.4 %scatter_custom_fusion.9 = f32[4097,2]{1,0:T(8,128)S(1)} fusion(s32[2048]{0:T(1024)S(1)} %get-tuple-element.177, f32[]{:T(128)} %constant.23.clone.1..sunk, f32[2,2048]{0,1:T(8,128)} %get-tuple-element.176, f32[2,2048]{0,1:T(8,128)S(1)} %get-tuple-element.163), kind=kCustom, calls=%fused_computation.5.clone.1 | custom fusion | flops 8192 | bytes 1097740 | tf_op jit(solution)/shard_map/while/body/eval_jaxpr/scatter-add | solution.py:85
  62.0 1.6 copy.127
  63.6 2.1 collective-permute-start
  65.7 3.4 subtract_add_fusion.2
  69.2 1.6 copy.128
  72.5 12.4 %scatter_custom_fusion.9 = f32[4097,2]{1,0:T(8,128)S(1)} fusion(s32[2048]{0:T(1024)S(1)} %get-tuple-element.177, f32[]{:T(128)} %constant.23.clone.1..sunk, f32[2,2048]{0,1:T(8,128)} %get-tuple-element.176, f32[2,2048]{0,1:T(8,128)S(1)} %get-tuple-element.163), kind=kCustom, calls=%fused_computation.5.clone.1 | custom fusion | flops 8192 | bytes 1097740 | tf_op jit(solution)/shard_map/while/body/eval_jaxpr/scatter-add | solution.py:85
  88.0 3.5 collective-permute-start
  91.6 3.4 subtract_add_fusion.2
  95.0 1.6 copy.128
  98.3 12.4 %scatter_custom_fusion.9 = f32[4097,2]{1,0:T(8,128)S(1)} fusion(s32[2048]{0:T(1024)S(1)} %get-tuple-element.177, f32[]{:T(128)} %constant.23.clone.1..sunk, f32[2,2048]{0,1:T(8,128)} %get-tuple-element.176, f32[2,2048]{0,1:T(8,128)S(1)} %get-tuple-element.163), kind=kCustom, calls=%fused_computation.5.clone.1 | custom fusion | flops 8192 | bytes 1097740 | tf_op jit(solution)/shard_map/while/body/eval_jaxpr/scatter-add | solution.py:85
  113.8 2.1 collective-permute-start
  115.9 3.4 subtract_add_fusion.2
  119.4 1.6 copy.128
  122.7 12.4 %scatter_custom_fusion.9 = f32[4097,2]{1,0:T(8,128)S(1)} fusion(s32[2048]{0:T(1024)S(1)} %get-tuple-element.177, f32[]{:T(128)} %constant.23.clone.1..sunk, f32[2,2048]{0,1:T(8,128)} %get-tuple-element.176, f32[2,2048]{0,1:T(8,128)S(1)} %get-tuple-element.163), kind=kCustom, calls=%fused_computation.5.clone.1 | custom fusion | flops 8192 | bytes 1097740 | tf_op jit(solution)/shard_map/while/body/eval_jaxpr/scatter-add | solution.py:85
  138.2 3.6 collective-permute-start
  141.8 3.4 subtract_add_fusion.2
  145.3 1.6 copy.128
  148.6 12.4 %scatter_custom_fusion.9 = f32[4097,2]{1,0:T(8,128)S(1)} fusion(s32[2048]{0:T(1024)S(1)} %get-tuple-element.177, f32[]{:T(128)} %constant.23.clone.1..sunk, f32[2,2048]{0,1:T(8,128)} %get-tuple-element.176, f32[2,2048]{0,1:T(8,128)S(1)} %get-tuple-element.163), kind=kCustom, calls=%fused_computation.5.clone.1 | custom fusion | flops 8192 | bytes 1097740 | tf_op jit(solution)/shard_map/while/body/eval_jaxpr/scatter-add | solution.py:85
  164.1 2.1 collective-permute-start
  166.2 3.4 subtract_add_fusion.2
  169.6 1.6 copy.128
  173.0 12.4 %scatter_custom_fusion.9 = f32[4097,2]{1,0:T(8,128)S(1)} fusion(s32[2048]{0:T(1024)S(1)} %get-tuple-element.177, f32[]{:T(128)} %constant.23.clone.1..sunk, f32[2,2048]{0,1:T(8,128)} %get-tuple-element.176, f32[2,2048]{0,1:T(8,128)S(1)} %get-tuple-element.163), kind=kCustom, calls=%fused_computation.5.clone.1 | custom fusion | flops 8192 | bytes 1097740 | tf_op jit(solution)/shard_map/while/body/eval_jaxpr/scatter-add | solution.py:85
  188.5 3.3 collective-permute-start
  191.8 3.4 subtract_add_fusion.2
  195.2 1.6 copy.128
  198.6 12.4 %scatter_custom_fusion.9 = f32[4097,2]{1,0:T(8,128)S(1)} fusion(s32[2048]{0:T(1024)S(1)} %get-tuple-element.177, f32[]{:T(128)} %constant.23.clone.1..sunk, f32[2,2048]{0,1:T(8,128)} %get-tuple-element.176, f32[2,2048]{0,1:T(8,128)S(1)} %get-tuple-element.163), kind=kCustom, calls=%fused_computation.5.clone.1 | custom fusion | flops 8192 | bytes 1097740 | tf_op jit(solution)/shard_map/while/body/eval_jaxpr/scatter-add | solution.py:85
  214.1 2.1 collective-permute-start
  216.2 3.4 subtract_add_fusion.2
  219.6 1.6 copy.128
  222.9 12.4 %scatter_custom_fusion.9 = f32[4097,2]{1,0:T(8,128)S(1)} fusion(s32[2048]{0:T(1024)S(1)} %get-tuple-element.177, f32[]{:T(128)} %constant.23.clone.1..sunk, f32[2,2048]{0,1:T(8,128)} %get-tuple-element.176, f32[2,2048]{0,1:T(8,128)S(1)} %get-tuple-element.163), kind=kCustom, calls=%fused_computation.5.clone.1 | custom fusion | flops 8192 | bytes 1097740 | tf_op jit(solution)/shard_map/while/body/eval_jaxpr/scatter-add | solution.py:85
  238.4 2.6 collective-permute-start
  241.1 3.4 subtract_add_fusion.2
  244.5 1.6 copy.128
  247.9 12.4 %scatter_custom_fusion.9 = f32[4097,2]{1,0:T(8,128)S(1)} fusion(s32[2048]{0:T(1024)S(1)} %get-tuple-element.177, f32[]{:T(128)} %constant.23.clone.1..sunk, f32[2,2048]{0,1:T(8,128)} %get-tuple-element.176, f32[2,2048]{0,1:T(8,128)S(1)} %get-tuple-element.163), kind=kCustom, calls=%fused_computation.5.clone.1 | custom fusion | flops 8192 | bytes 1097740 | tf_op jit(solution)/shard_map/while/body/eval_jaxpr/scatter-add | solution.py:85
  263.4 2.1 collective-permute-start
  265.4 3.4 subtract_add_fusion.2
  268.9 1.6 copy.128
  272.2 12.4 %scatter_custom_fusion.9 = f32[4097,2]{1,0:T(8,128)S(1)} fusion(s32[2048]{0:T(1024)S(1)} %get-tuple-element.177, f32[]{:T(128)} %constant.23.clone.1..sunk, f32[2,2048]{0,1:T(8,128)} %get-tuple-element.176, f32[2,2048]{0,1:T(8,128)S(1)} %get-tuple-element.163), kind=kCustom, calls=%fused_computation.5.clone.1 | custom fusion | flops 8192 | bytes 1097740 | tf_op jit(solution)/shard_map/while/body/eval_jaxpr/scatter-add | solution.py:85
  287.7 3.6 collective-permute-start
  291.3 3.4 subtract_add_fusion.2
  294.8 1.6 copy.128
  298.1 12.4 %scatter_custom_fusion.9 = f32[4097,2]{1,0:T(8,128)S(1)} fusion(s32[2048]{0:T(1024)S(1)} %get-tuple-element.177, f32[]{:T(128)} %constant.23.clone.1..sunk, f32[2,2048]{0,1:T(8,128)} %get-tuple-element.176, f32[2,2048]{0,1:T(8,128)S(1)} %get-tuple-element.163), kind=kCustom, calls=%fused_computation.5.clone.1 | custom fusion | flops 8192 | bytes 1097740 | tf_op jit(solution)/shard_map/while/body/eval_jaxpr/scatter-add | solution.py:85
  313.6 2.0 collective-permute-start
  315.7 3.4 subtract_add_fusion.2
  319.1 1.6 copy.128
  322.5 12.4 %scatter_custom_fusion.9 = f32[4097,2]{1,0:T(8,128)S(1)} fusion(s32[2048]{0:T(1024)S(1)} %get-tuple-element.177, f32[]{:T(128)} %constant.23.clone.1..sunk, f32[2,2048]{0,1:T(8,128)} %get-tuple-element.176, f32[2,2048]{0,1:T(8,128)S(1)} %get-tuple-element.163), kind=kCustom, calls=%fused_computation.5.clone.1 | custom fusion | flops 8192 | bytes 1097740 | tf_op jit(solution)/shard_map/while/body/eval_jaxpr/scatter-add | solution.py:85
  338.0 3.6 collective-permute-start
  341.6 3.4 subtract_add_fusion.2
  345.0 1.6 copy.128
  349.1 6.2 %gather_fusion.1 = f32[1024]{0:T(1024)S(1)} fusion(f32[2048]{0:T(1024)S(1)} %add_divide_fusion, s32[1024]{0:T(1024)S(1)} %get-tuple-element.75), kind=kCustom, calls=%fused_computation.1 | custom fusion | bytes 12288 | tf_op jit(solution)/shard_map/gather | solution.py:139
  356.0 10.4 %all-to-all-start.1 = ((f32[4,32,8]{2,0,1:T(4,128)}), f32[4,32,8]{2,0,1:T(4,128)S(1)}, u32[]{:S(2)}, u32[]{:S(2)}) async-start(f32[4,32,8]{2,0,1:T(4,128)} %copy.90), calls=%async_computation.1 | async-start | bytes 131072 | tf_op jit(solution)/shard_map/all_to_all | solution.py:141
  366.4 2.5 fusion.27
  376.9 4.0 all-to-all-start.2
  381.5 4.7 %all-to-all-done.2 = f32[4,1,256]{2,1,0:T(1,128)S(1)} async-done(((f32[4,1,256]{2,1,0:T(1,128)}), f32[4,1,256]{2,1,0:T(1,128)S(1)}, u32[]{:S(2)}, u32[]{:S(2)}) %all-to-all-start.2) | async-done | bytes 4128 | tf_op jit(solution)/shard_map/all_to_all | solution.py:140
  386.2 7.6 %scatter_custom_fusion.2 = f32[129]{0:T(256)S(1)} fusion(s32[1024]{0:T(1024)S(1)} %get-tuple-element.80, f32[1024]{0:T(1024)S(1)} %mul.247, f32[]{:T(128)} %constant.23.clone.1), kind=kCustom, calls=%fused_computation.78 | custom fusion | flops 1024 | bytes 520 | tf_op jit(solution)/shard_map/scatter-add | solution.py:149
  393.9 4.9 %fusion.5 = f32[48,64,128]{2,1,0:T(8,128)} fusion(f32[6,8,64,128]{3,2,1,0:T(8,128)} %copy.104, f32[6,8,64,128]{3,2,1,0:T(8,128)} %copy.103, f32[6,8,64,128]{3,2,1,0:T(8,128)} %copy.102, f32[6,8,64,128]{3,2,1,0:T(8,128)} %copy.101, f32[64,128]{1,0:T(8,128)S(1)} %multiply_exponential_fusion, f32[128]{0:T(128)S(1)} %get-tuple-element.86, ...), kind=kLoop, calls=%fused_computation.14 | loop fusion | flops 3145728 | bytes 7899136 | tf_op jit(solution)/shard_map/mul | solution.py:154
  (251 shorter events, 78.4 us)
Async XLA Ops:
  3.5 3.7 copy-start.12
  3.5 3.7 copy-start.18
  3.5 3.9 copy-start.14
  7.2 23.1 %copy-start.4 = (f32[48,64,128]{2,1,0:T(8,128)}, f32[48,64,128]{2,1,0:T(8,128)S(1)}, u32[]{:S(2)}) copy-start(f32[48,64,128]{2,1,0:T(8,128)S(1)} %get-tuple-element.70) | copy-start | bytes 4718596
  7.2 15.6 %copy-start.9 = (f32[4,48,48]{2,1,0:T(8,128)S(1)}, f32[4,48,48]{2,1,0:T(8,128)}, u32[]{:S(2)}) copy-start(f32[4,48,48]{2,1,0:T(8,128)} %param.20) | copy-start | bytes 110596
  12.3 26.1 %all-to-all-start = ((f32[128,3,1,8]{3,2,1,0:T(1,128)}), f32[128,3,1,8]{3,2,1,0:T(1,128)S(1)}, u32[]{:S(2)}, u32[]{:S(2)}) async-start(f32[128,3,1,8]{3,2,1,0:T(1,128)} %bitcast.27), calls=%async_computation | async-start | bytes 393216 | tf_op jit(solution)/shard_map/all_to_all | solution.py:27
  26.5 3.7 copy-start.13
  26.5 3.7 copy-start.10
  26.5 3.7 copy-start.11
  26.5 3.7 copy-start.16
  26.5 3.7 copy-start.17
  62.0 3.7 copy-start
  63.6 7.8 %collective-permute-start = (f32[2,2048]{1,0:T(2,128)S(1)}, f32[2,2048]{1,0:T(2,128)S(1)}, u32[]{:S(2)}, u32[]{:S(2)}) collective-permute-start(f32[2,2048]{1,0:T(2,128)S(1)} %copy.127), channel_id=1, source_target_pairs={{0,1},{1,2},{2,3},{3,4},{4,5},{5,6},{6,7},{7,8},{8,9},{9,10},{10,1... | collective-permute-start | bytes 49160 | tf_op jit(solution)/shard_map/while/body/eval_jaxpr/ppermute | solution.py:35
  69.2 2.0 copy-start.1
  71.1 1.2 copy-start.3
  86.4 5.2 %copy-start = (f32[2,2048]{0,1:T(8,128)S(1)}, f32[2,2048]{0,1:T(8,128)}, u32[]{:S(2)}) copy-start(f32[2,2048]{0,1:T(8,128)} %get-tuple-element.176) | copy-start | bytes 49156 | tf_op jit(solution)/shard_map/while
  88.0 9.3 %collective-permute-start = (f32[2,2048]{1,0:T(2,128)S(1)}, f32[2,2048]{1,0:T(2,128)S(1)}, u32[]{:S(2)}, u32[]{:S(2)}) collective-permute-start(f32[2,2048]{1,0:T(2,128)S(1)} %copy.127), channel_id=1, source_target_pairs={{0,1},{1,2},{2,3},{3,4},{4,5},{5,6},{6,7},{7,8},{8,9},{9,10},{10,1... | collective-permute-start | bytes 49160 | tf_op jit(solution)/shard_map/while/body/eval_jaxpr/ppermute | solution.py:35
  95.0 2.0 copy-start.1
  97.0 1.2 copy-start.3
  112.2 3.7 copy-start
  113.8 7.9 %collective-permute-start = (f32[2,2048]{1,0:T(2,128)S(1)}, f32[2,2048]{1,0:T(2,128)S(1)}, u32[]{:S(2)}, u32[]{:S(2)}) collective-permute-start(f32[2,2048]{1,0:T(2,128)S(1)} %copy.127), channel_id=1, source_target_pairs={{0,1},{1,2},{2,3},{3,4},{4,5},{5,6},{6,7},{7,8},{8,9},{9,10},{10,1... | collective-permute-start | bytes 49160 | tf_op jit(solution)/shard_map/while/body/eval_jaxpr/ppermute | solution.py:35
  119.4 2.0 copy-start.1
  136.6 5.3 %copy-start = (f32[2,2048]{0,1:T(8,128)S(1)}, f32[2,2048]{0,1:T(8,128)}, u32[]{:S(2)}) copy-start(f32[2,2048]{0,1:T(8,128)} %get-tuple-element.176) | copy-start | bytes 49156 | tf_op jit(solution)/shard_map/while
  138.2 9.4 %collective-permute-start = (f32[2,2048]{1,0:T(2,128)S(1)}, f32[2,2048]{1,0:T(2,128)S(1)}, u32[]{:S(2)}, u32[]{:S(2)}) collective-permute-start(f32[2,2048]{1,0:T(2,128)S(1)} %copy.127), channel_id=1, source_target_pairs={{0,1},{1,2},{2,3},{3,4},{4,5},{5,6},{6,7},{7,8},{8,9},{9,10},{10,1... | collective-permute-start | bytes 49160 | tf_op jit(solution)/shard_map/while/body/eval_jaxpr/ppermute | solution.py:35
  145.3 2.0 copy-start.1
  147.2 1.2 copy-start.3
  162.5 3.7 copy-start
  164.1 7.9 %collective-permute-start = (f32[2,2048]{1,0:T(2,128)S(1)}, f32[2,2048]{1,0:T(2,128)S(1)}, u32[]{:S(2)}, u32[]{:S(2)}) collective-permute-start(f32[2,2048]{1,0:T(2,128)S(1)} %copy.127), channel_id=1, source_target_pairs={{0,1},{1,2},{2,3},{3,4},{4,5},{5,6},{6,7},{7,8},{8,9},{9,10},{10,1... | collective-permute-start | bytes 49160 | tf_op jit(solution)/shard_map/while/body/eval_jaxpr/ppermute | solution.py:35
  169.6 2.0 copy-start.1
  171.6 1.2 copy-start.3
  186.8 5.0 %copy-start = (f32[2,2048]{0,1:T(8,128)S(1)}, f32[2,2048]{0,1:T(8,128)}, u32[]{:S(2)}) copy-start(f32[2,2048]{0,1:T(8,128)} %get-tuple-element.176) | copy-start | bytes 49156 | tf_op jit(solution)/shard_map/while
  188.5 9.1 %collective-permute-start = (f32[2,2048]{1,0:T(2,128)S(1)}, f32[2,2048]{1,0:T(2,128)S(1)}, u32[]{:S(2)}, u32[]{:S(2)}) collective-permute-start(f32[2,2048]{1,0:T(2,128)S(1)} %copy.127), channel_id=1, source_target_pairs={{0,1},{1,2},{2,3},{3,4},{4,5},{5,6},{6,7},{7,8},{8,9},{9,10},{10,1... | collective-permute-start | bytes 49160 | tf_op jit(solution)/shard_map/while/body/eval_jaxpr/ppermute | solution.py:35
  195.2 2.0 copy-start.1
  212.4 3.7 copy-start
  214.1 7.8 %collective-permute-start = (f32[2,2048]{1,0:T(2,128)S(1)}, f32[2,2048]{1,0:T(2,128)S(1)}, u32[]{:S(2)}, u32[]{:S(2)}) collective-permute-start(f32[2,2048]{1,0:T(2,128)S(1)} %copy.127), channel_id=1, source_target_pairs={{0,1},{1,2},{2,3},{3,4},{4,5},{5,6},{6,7},{7,8},{8,9},{9,10},{10,1... | collective-permute-start | bytes 49160 | tf_op jit(solution)/shard_map/while/body/eval_jaxpr/ppermute | solution.py:35
  219.6 2.0 copy-start.1
  221.6 1.2 copy-start.3
  236.8 4.3 %copy-start = (f32[2,2048]{0,1:T(8,128)S(1)}, f32[2,2048]{0,1:T(8,128)}, u32[]{:S(2)}) copy-start(f32[2,2048]{0,1:T(8,128)} %get-tuple-element.176) | copy-start | bytes 49156 | tf_op jit(solution)/shard_map/while
  238.4 8.4 %collective-permute-start = (f32[2,2048]{1,0:T(2,128)S(1)}, f32[2,2048]{1,0:T(2,128)S(1)}, u32[]{:S(2)}, u32[]{:S(2)}) collective-permute-start(f32[2,2048]{1,0:T(2,128)S(1)} %copy.127), channel_id=1, source_target_pairs={{0,1},{1,2},{2,3},{3,4},{4,5},{5,6},{6,7},{7,8},{8,9},{9,10},{10,1... | collective-permute-start | bytes 49160 | tf_op jit(solution)/shard_map/while/body/eval_jaxpr/ppermute | solution.py:35
  244.5 2.0 copy-start.1
  246.5 1.2 copy-start.3
  261.7 3.7 copy-start
  263.4 7.9 %collective-permute-start = (f32[2,2048]{1,0:T(2,128)S(1)}, f32[2,2048]{1,0:T(2,128)S(1)}, u32[]{:S(2)}, u32[]{:S(2)}) collective-permute-start(f32[2,2048]{1,0:T(2,128)S(1)} %copy.127), channel_id=1, source_target_pairs={{0,1},{1,2},{2,3},{3,4},{4,5},{5,6},{6,7},{7,8},{8,9},{9,10},{10,1... | collective-permute-start | bytes 49160 | tf_op jit(solution)/shard_map/while/body/eval_jaxpr/ppermute | solution.py:35
  268.9 2.0 copy-start.1
  270.9 1.2 copy-start.3
  286.1 5.2 %copy-start = (f32[2,2048]{0,1:T(8,128)S(1)}, f32[2,2048]{0,1:T(8,128)}, u32[]{:S(2)}) copy-start(f32[2,2048]{0,1:T(8,128)} %get-tuple-element.176) | copy-start | bytes 49156 | tf_op jit(solution)/shard_map/while
  287.7 9.4 %collective-permute-start = (f32[2,2048]{1,0:T(2,128)S(1)}, f32[2,2048]{1,0:T(2,128)S(1)}, u32[]{:S(2)}, u32[]{:S(2)}) collective-permute-start(f32[2,2048]{1,0:T(2,128)S(1)} %copy.127), channel_id=1, source_target_pairs={{0,1},{1,2},{2,3},{3,4},{4,5},{5,6},{6,7},{7,8},{8,9},{9,10},{10,1... | collective-permute-start | bytes 49160 | tf_op jit(solution)/shard_map/while/body/eval_jaxpr/ppermute | solution.py:35
  294.8 2.0 copy-start.1
  296.8 1.2 copy-start.3
  312.0 3.7 copy-start
  313.6 7.8 %collective-permute-start = (f32[2,2048]{1,0:T(2,128)S(1)}, f32[2,2048]{1,0:T(2,128)S(1)}, u32[]{:S(2)}, u32[]{:S(2)}) collective-permute-start(f32[2,2048]{1,0:T(2,128)S(1)} %copy.127), channel_id=1, source_target_pairs={{0,1},{1,2},{2,3},{3,4},{4,5},{5,6},{6,7},{7,8},{8,9},{9,10},{10,1... | collective-permute-start | bytes 49160 | tf_op jit(solution)/shard_map/while/body/eval_jaxpr/ppermute | solution.py:35
  319.1 2.0 copy-start.1
  321.1 1.2 copy-start.3
  336.3 5.3 %copy-start = (f32[2,2048]{0,1:T(8,128)S(1)}, f32[2,2048]{0,1:T(8,128)}, u32[]{:S(2)}) copy-start(f32[2,2048]{0,1:T(8,128)} %get-tuple-element.176) | copy-start | bytes 49156 | tf_op jit(solution)/shard_map/while
  338.0 9.4 %collective-permute-start = (f32[2,2048]{1,0:T(2,128)S(1)}, f32[2,2048]{1,0:T(2,128)S(1)}, u32[]{:S(2)}, u32[]{:S(2)}) collective-permute-start(f32[2,2048]{1,0:T(2,128)S(1)} %copy.127), channel_id=1, source_target_pairs={{0,1},{1,2},{2,3},{3,4},{4,5},{5,6},{6,7},{7,8},{8,9},{9,10},{10,1... | collective-permute-start | bytes 49160 | tf_op jit(solution)/shard_map/while/body/eval_jaxpr/ppermute | solution.py:35
  345.0 2.0 copy-start.1
  349.1 17.3 %copy-start.5 = (f32[48,64,128]{2,1,0:T(8,128)S(1)}, f32[48,64,128]{2,1,0:T(8,128)}, u32[]{:S(2)}) copy-start(f32[48,64,128]{2,1,0:T(8,128)} %copy-done.4) | copy-start | bytes 4718596
  356.0 20.2 %all-to-all-start.1 = ((f32[4,32,8]{2,0,1:T(4,128)}), f32[4,32,8]{2,0,1:T(4,128)S(1)}, u32[]{:S(2)}, u32[]{:S(2)}) async-start(f32[4,32,8]{2,0,1:T(4,128)} %copy.90), calls=%async_computation.1 | async-start | bytes 131072 | tf_op jit(solution)/shard_map/all_to_all | solution.py:141
  366.4 2.5 copy-start.7
  368.9 1.8 copy-start.6
  370.8 1.9 copy-start.8
  374.1 1.8 copy-start.2
  376.9 9.2 %all-to-all-start.2 = ((f32[4,1,256]{2,1,0:T(1,128)}), f32[4,1,256]{2,1,0:T(1,128)S(1)}, u32[]{:S(2)}, u32[]{:S(2)}) async-start(f32[4,1,256]{2,1,0:T(1,128)} %all_to_all.20), calls=%async_computation.2 | async-start | bytes 8192 | tf_op jit(solution)/shard_map/all_to_all | solution.py:140
  393.8 5.0 %copy-start.19 = (f32[128]{0:T(128)}, f32[128]{0:T(128)S(1)}, u32[]{:S(2)}) copy-start(f32[128]{0:T(128)S(1)} %slice.114) | copy-start | bytes 1540
  (4 other events, 4.4 us)
where the time goes:
time: 401 us; the launch traced here: 399 us
  other arithmetic  217 us (54%)
  local copies, waits for them, and re-layouts  101 us (25%)
  starting transfers between devices  57.4 us (14%)
  matrix products  17.1 us (4%)
  waiting for transfers between devices  4.7 us (1%)
    scatter-add x12, other arithmetic, scatter_pair(): return jax.ops.segment_sum(outflow.T, slots, num_segments=segments).T  149 us
    add x12, other arithmetic, substep(): hill_water - hill_out + surface_in  41.2 us
    slice x24, local copies, waits for them, and re-layouts, substep(): from_above = from_behind(spread[:, rivers:2 * rivers], ('comp', 'cell'), 1)  36.8 us
    ppermute x12, starting transfers between devices, from_behind(): lax.ppermute(value, axis, [(source, source + steps) for source in range(i...  32.6 us
    sub x12, local copies, waits for them, and re-layouts, substep(): channel - outflow + hill_out + inflow + deep_in  19.7 us
    dot_general x4, matrix products, transit(): jnp.dot(transitions[kind_index], flat_mass, precision=highest, preferred_...  13.5 us
    unnamed x42, local copies, waits for them, and re-layouts  11.2 us
    all_to_all x1, starting transfers between devices, joined_exchange(): lax.all_to_all(blocks, axis, split_axis=0, concat_axis=0, tiled=True)  10.5 us
  transfers between devices with their start and end apart: 15, of which 1 were waited for; matrix products, arithmetic and copies ran while one was open for 24% of the time, Pallas kernels for 0%

commit v1 on v0

--- a/solution.py
+++ b/solution.py
@@ -137,10 +137,21 @@
     stored_total = channel[0] + channel[1]
     inundation = stored_total / (stored_total + capacity)
     flood_back = jnp.where(has_target, inundation[jnp.where(has_target, river_target, 0)], 0.0)
+
+    def bars_make(in_array):
+        outcome_arr = jnp.concatenate(
+            jax.lax.all_to_all(
+                jnp.stack(jnp.split(in_array, jax.lax.axis_size("cell"), axis=1), axis=0),
+                "cell",
+                0,
+                0,
+            ),
+            axis=1,
+        )
+        return outcome_arr
+
     returned = lax.all_to_all(
-        lax.all_to_all(
-            flood_back.reshape(comp_parts, -1), "cell", split_axis=1, concat_axis=1, tiled=True
-        ),
+        bars_make(flood_back.reshape(comp_parts, -1)),
         "comp",
         split_axis=0,
         concat_axis=0,

time: 401 us -> 420 us (1.047)
  local copies, waits for them, and re-layouts: 101 us -> 121 us
    unnamed x42 -> x75, local copies, waits for them, and re-layouts: 11.2 us -> 31.3 us
  transfers between devices with their start and end apart: 15 -> 15, of which waited for: 1 -> 1; matrix products, arithmetic and copies ran while one was open for 24% -> 23% of each run, Pallas kernels for 0% -> 0%
where the time goes in v1:
time: 420 us; the launch traced here: 417 us
  other arithmetic  216 us (51%)
  local copies, waits for them, and re-layouts  121 us (29%)
  starting transfers between devices  57.4 us (14%)
  matrix products  17.1 us (4%)
  waiting for transfers between devices  4.7 us (1%)
    scatter-add x12, other arithmetic, scatter_pair(): return jax.ops.segment_sum(outflow.T, slots, num_segments=segments).T  149 us
    add x12, other arithmetic, substep(): hill_water - hill_out + surface_in  41.2 us
    slice x24, local copies, waits for them, and re-layouts, substep(): from_above = from_behind(spread[:, rivers:2 * rivers], ('comp', 'cell'), 1)  36.8 us
    ppermute x12, starting transfers between devices, from_behind(): lax.ppermute(value, axis, [(source, source + steps) for source in range(i...  32.6 us
    unnamed x75, local copies, waits for them, and re-layouts  31.3 us
    sub x12, local copies, waits for them, and re-layouts, substep(): channel - outflow + hill_out + inflow + deep_in  19.7 us
    dot_general x4, matrix products, transit(): jnp.dot(transitions[kind_index], flat_mass, precision=highest, preferred_...  13.5 us
    all_to_all x1, starting transfers between devices, joined_exchange(): lax.all_to_all(blocks, axis, split_axis=0, concat_axis=0, tiled=True)  10.5 us
  transfers between devices with their start and end apart: 15, of which 1 were waited for; matrix products, arithmetic and copies ran while one was open for 23% of the time, Pallas kernels for 0%

profile of v1, /device:TPU:8, one launch (start us, length us, event | category | flops | bytes accessed | tf_op | source)
XLA Modules:
  0.0 417.5 jit_solution(5937459440676506805)
XLA Ops:
  2.2 3.6 fusion.52
  6.1 2.8 gather_fusion
  11.0 10.5 %all-to-all-start = ((f32[128,3,1,8]{3,2,1,0:T(1,128)}), f32[128,3,1,8]{3,2,1,0:T(1,128)S(1)}, u32[]{:S(2)}, u32[]{:S(2)}) async-start(f32[128,3,1,8]{3,2,1,0:T(1,128)} %bitcast.27), calls=%async_computation | async-start | bytes 393216 | tf_op jit(solution)/shard_map/all_to_all | solution.py:27
  21.5 3.7 fusion.18
  25.2 3.6 fusion.21
  28.9 3.7 fusion.24
  37.8 6.5 %scatter_custom_fusion.1 = f32[2049,3]{1,0:T(8,128)S(1)} fusion(s32[1024]{0:T(1024)S(1)} %get-tuple-element.76, f32[1024,3]{1,0:T(8,128)S(1)} %copy.254, f32[]{:T(128)} %constant.23.clone.1), kind=kCustom, calls=%fused_computation.45 | custom fusion | flops 3072 | bytes 24592 | tf_op jit(solution)/shard_map/scatter-add | solution.py:118
  46.8 300.2 %while.12 = (s32[]{:T(128)}, f32[2,2048]{0,1:T(8,128)}, f32[2,2048]{0,1:T(8,128)S(1)}, f32[2,2048]{0,1:T(8,128)}, f32[2,2048]{0,1:T(8,128)}, /*index=5*/f32[2,20...) while((s32[]{:T(128)}, f32[2,2048]{0,1:T(8,128)}, f32[2,2048]{0,1:T(8,128)S(1)}, ...), condition=%wide.region_5.6_spmd, body=%wide.region_3.5_spmd.sunk | while | flops 45058 | bytes 1851629 | solution.py:136
  46.8 12.4 %scatter_custom_fusion.9 = f32[4097,2]{1,0:T(8,128)S(1)} fusion(s32[2048]{0:T(1024)S(1)} %get-tuple-element.179, f32[]{:T(128)} %constant.23.clone.1..sunk, f32[2,2048]{0,1:T(8,128)} %get-tuple-element.178, f32[2,2048]{0,1:T(8,128)S(1)} %get-tuple-element.165), kind=kCustom, calls=%fused_computation.5.clone.1 | custom fusion | flops 8192 | bytes 1097740 | tf_op jit(solution)/shard_map/while/body/eval_jaxpr/scatter-add | solution.py:85
  60.7 1.6 copy.292
  62.3 2.1 collective-permute-start
  64.4 3.4 subtract_add_fusion.2
  67.8 1.6 copy.293
  71.2 12.4 %scatter_custom_fusion.9 = f32[4097,2]{1,0:T(8,128)S(1)} fusion(s32[2048]{0:T(1024)S(1)} %get-tuple-element.179, f32[]{:T(128)} %constant.23.clone.1..sunk, f32[2,2048]{0,1:T(8,128)} %get-tuple-element.178, f32[2,2048]{0,1:T(8,128)S(1)} %get-tuple-element.165), kind=kCustom, calls=%fused_computation.5.clone.1 | custom fusion | flops 8192 | bytes 1097740 | tf_op jit(solution)/shard_map/while/body/eval_jaxpr/scatter-add | solution.py:85
  86.7 3.5 collective-permute-start
  90.2 3.4 subtract_add_fusion.2
  93.7 1.6 copy.293
  97.0 12.4 %scatter_custom_fusion.9 = f32[4097,2]{1,0:T(8,128)S(1)} fusion(s32[2048]{0:T(1024)S(1)} %get-tuple-element.179, f32[]{:T(128)} %constant.23.clone.1..sunk, f32[2,2048]{0,1:T(8,128)} %get-tuple-element.178, f32[2,2048]{0,1:T(8,128)S(1)} %get-tuple-element.165), kind=kCustom, calls=%fused_computation.5.clone.1 | custom fusion | flops 8192 | bytes 1097740 | tf_op jit(solution)/shard_map/while/body/eval_jaxpr/scatter-add | solution.py:85
  112.5 2.1 collective-permute-start
  114.6 3.4 subtract_add_fusion.2
  118.0 1.6 copy.293
  121.4 12.4 %scatter_custom_fusion.9 = f32[4097,2]{1,0:T(8,128)S(1)} fusion(s32[2048]{0:T(1024)S(1)} %get-tuple-element.179, f32[]{:T(128)} %constant.23.clone.1..sunk, f32[2,2048]{0,1:T(8,128)} %get-tuple-element.178, f32[2,2048]{0,1:T(8,128)S(1)} %get-tuple-element.165), kind=kCustom, calls=%fused_computation.5.clone.1 | custom fusion | flops 8192 | bytes 1097740 | tf_op jit(solution)/shard_map/while/body/eval_jaxpr/scatter-add | solution.py:85
  136.9 3.6 collective-permute-start
  140.5 3.4 subtract_add_fusion.2
  143.9 1.6 copy.293
  147.3 12.4 %scatter_custom_fusion.9 = f32[4097,2]{1,0:T(8,128)S(1)} fusion(s32[2048]{0:T(1024)S(1)} %get-tuple-element.179, f32[]{:T(128)} %constant.23.clone.1..sunk, f32[2,2048]{0,1:T(8,128)} %get-tuple-element.178, f32[2,2048]{0,1:T(8,128)S(1)} %get-tuple-element.165), kind=kCustom, calls=%fused_computation.5.clone.1 | custom fusion | flops 8192 | bytes 1097740 | tf_op jit(solution)/shard_map/while/body/eval_jaxpr/scatter-add | solution.py:85
  162.8 2.1 collective-permute-start
  164.9 3.4 subtract_add_fusion.2
  168.3 1.6 copy.293
  171.6 12.4 %scatter_custom_fusion.9 = f32[4097,2]{1,0:T(8,128)S(1)} fusion(s32[2048]{0:T(1024)S(1)} %get-tuple-element.179, f32[]{:T(128)} %constant.23.clone.1..sunk, f32[2,2048]{0,1:T(8,128)} %get-tuple-element.178, f32[2,2048]{0,1:T(8,128)S(1)} %get-tuple-element.165), kind=kCustom, calls=%fused_computation.5.clone.1 | custom fusion | flops 8192 | bytes 1097740 | tf_op jit(solution)/shard_map/while/body/eval_jaxpr/scatter-add | solution.py:85
  187.1 3.3 collective-permute-start
  190.5 3.4 subtract_add_fusion.2
  193.9 1.6 copy.293
  197.2 12.4 %scatter_custom_fusion.9 = f32[4097,2]{1,0:T(8,128)S(1)} fusion(s32[2048]{0:T(1024)S(1)} %get-tuple-element.179, f32[]{:T(128)} %constant.23.clone.1..sunk, f32[2,2048]{0,1:T(8,128)} %get-tuple-element.178, f32[2,2048]{0,1:T(8,128)S(1)} %get-tuple-element.165), kind=kCustom, calls=%fused_computation.5.clone.1 | custom fusion | flops 8192 | bytes 1097740 | tf_op jit(solution)/shard_map/while/body/eval_jaxpr/scatter-add | solution.py:85
  212.7 2.1 collective-permute-start
  214.8 3.4 subtract_add_fusion.2
  218.3 1.6 copy.293
  221.6 12.4 %scatter_custom_fusion.9 = f32[4097,2]{1,0:T(8,128)S(1)} fusion(s32[2048]{0:T(1024)S(1)} %get-tuple-element.179, f32[]{:T(128)} %constant.23.clone.1..sunk, f32[2,2048]{0,1:T(8,128)} %get-tuple-element.178, f32[2,2048]{0,1:T(8,128)S(1)} %get-tuple-element.165), kind=kCustom, calls=%fused_computation.5.clone.1 | custom fusion | flops 8192 | bytes 1097740 | tf_op jit(solution)/shard_map/while/body/eval_jaxpr/scatter-add | solution.py:85
  237.1 2.6 collective-permute-start
  239.7 3.4 subtract_add_fusion.2
  243.2 1.6 copy.293
  246.5 12.4 %scatter_custom_fusion.9 = f32[4097,2]{1,0:T(8,128)S(1)} fusion(s32[2048]{0:T(1024)S(1)} %get-tuple-element.179, f32[]{:T(128)} %constant.23.clone.1..sunk, f32[2,2048]{0,1:T(8,128)} %get-tuple-element.178, f32[2,2048]{0,1:T(8,128)S(1)} %get-tuple-element.165), kind=kCustom, calls=%fused_computation.5.clone.1 | custom fusion | flops 8192 | bytes 1097740 | tf_op jit(solution)/shard_map/while/body/eval_jaxpr/scatter-add | solution.py:85
  262.0 2.1 collective-permute-start
  264.1 3.4 subtract_add_fusion.2
  267.6 1.6 copy.293
  270.9 12.4 %scatter_custom_fusion.9 = f32[4097,2]{1,0:T(8,128)S(1)} fusion(s32[2048]{0:T(1024)S(1)} %get-tuple-element.179, f32[]{:T(128)} %constant.23.clone.1..sunk, f32[2,2048]{0,1:T(8,128)} %get-tuple-element.178, f32[2,2048]{0,1:T(8,128)S(1)} %get-tuple-element.165), kind=kCustom, calls=%fused_computation.5.clone.1 | custom fusion | flops 8192 | bytes 1097740 | tf_op jit(solution)/shard_map/while/body/eval_jaxpr/scatter-add | solution.py:85
  286.4 3.6 collective-permute-start
  290.0 3.4 subtract_add_fusion.2
  293.4 1.6 copy.293
  296.8 12.4 %scatter_custom_fusion.9 = f32[4097,2]{1,0:T(8,128)S(1)} fusion(s32[2048]{0:T(1024)S(1)} %get-tuple-element.179, f32[]{:T(128)} %constant.23.clone.1..sunk, f32[2,2048]{0,1:T(8,128)} %get-tuple-element.178, f32[2,2048]{0,1:T(8,128)S(1)} %get-tuple-element.165), kind=kCustom, calls=%fused_computation.5.clone.1 | custom fusion | flops 8192 | bytes 1097740 | tf_op jit(solution)/shard_map/while/body/eval_jaxpr/scatter-add | solution.py:85
  312.3 2.1 collective-permute-start
  314.4 3.4 subtract_add_fusion.2
  317.8 1.6 copy.293
  321.1 12.4 %scatter_custom_fusion.9 = f32[4097,2]{1,0:T(8,128)S(1)} fusion(s32[2048]{0:T(1024)S(1)} %get-tuple-element.179, f32[]{:T(128)} %constant.23.clone.1..sunk, f32[2,2048]{0,1:T(8,128)} %get-tuple-element.178, f32[2,2048]{0,1:T(8,128)S(1)} %get-tuple-element.165), kind=kCustom, calls=%fused_computation.5.clone.1 | custom fusion | flops 8192 | bytes 1097740 | tf_op jit(solution)/shard_map/while/body/eval_jaxpr/scatter-add | solution.py:85
  336.6 3.6 collective-permute-start
  340.3 3.4 subtract_add_fusion.2
  343.7 1.6 copy.293
  347.8 6.2 %gather_fusion.1 = f32[1024]{0:T(1024)S(1)} fusion(f32[2048]{0:T(1024)S(1)} %add_divide_fusion, s32[1024]{0:T(1024)S(1)} %get-tuple-element.75), kind=kCustom, calls=%fused_computation.1 | custom fusion | bytes 12288 | tf_op jit(solution)/shard_map/gather | solution.py:139
  374.7 10.4 %all-to-all-start.1 = ((f32[32,4,8]{2,1,0:T(4,128)}), f32[32,4,8]{2,1,0:T(4,128)S(1)}, u32[]{:S(2)}, u32[]{:S(2)}) async-start(f32[32,4,8]{2,1,0:T(4,128)} %constant_dynamic-update-slice_fusion), calls=%async_computation.1 | async-start | bytes 131072 | tf_op jit(solution)/shard_map/all_to_all | solution.py:143
  385.1 2.5 fusion.27
  395.6 3.9 all-to-all-start.2
  400.2 4.7 %all-to-all-done.2 = f32[4,1,256]{2,1,0:T(1,128)S(1)} async-done(((f32[4,1,256]{2,1,0:T(1,128)}), f32[4,1,256]{2,1,0:T(1,128)S(1)}, u32[]{:S(2)}, u32[]{:S(2)}) %all-to-all-start.2) | async-done | bytes 4128 | tf_op jit(solution)/shard_map/all_to_all | solution.py:153
  404.9 7.6 %scatter_custom_fusion.2 = f32[129]{0:T(256)S(1)} fusion(s32[1024]{0:T(1024)S(1)} %get-tuple-element.92, f32[1024]{0:T(1024)S(1)} %mul.247, f32[]{:T(128)} %constant.23.clone.1), kind=kCustom, calls=%fused_computation.142 | custom fusion | flops 1024 | bytes 520 | tf_op jit(solution)/shard_map/scatter-add | solution.py:160
  412.6 4.9 %fusion.5 = f32[48,64,128]{2,1,0:T(8,128)} fusion(f32[6,8,64,128]{3,2,1,0:T(8,128)} %copy.269, f32[6,8,64,128]{3,2,1,0:T(8,128)} %copy.268, f32[6,8,64,128]{3,2,1,0:T(8,128)} %copy.267, f32[6,8,64,128]{3,2,1,0:T(8,128)} %copy.266, f32[64,128]{1,0:T(8,128)S(1)} %multiply_exponential_fusion, f32[128]{0:T(128)S(1)} %get-tuple-element.86, ...), kind=kLoop, calls=%fused_computation.14 | loop fusion | flops 3145728 | bytes 7899136 | tf_op jit(solution)/shard_map/mul | solution.py:165
  (283 shorter events, 97.0 us)
Async XLA Ops:
  2.2 3.7 copy-start.12
  2.2 3.7 copy-start.19
  2.2 3.9 copy-start.15
  2.2 3.9 copy-start.14
  2.2 3.9 copy-start.13
  5.8 23.1 %copy-start.4 = (f32[48,64,128]{2,1,0:T(8,128)}, f32[48,64,128]{2,1,0:T(8,128)S(1)}, u32[]{:S(2)}) copy-start(f32[48,64,128]{2,1,0:T(8,128)S(1)} %get-tuple-element.70) | copy-start | bytes 4718596
  5.8 15.7 %copy-start.9 = (f32[4,48,48]{2,1,0:T(8,128)S(1)}, f32[4,48,48]{2,1,0:T(8,128)}, u32[]{:S(2)}) copy-start(f32[4,48,48]{2,1,0:T(8,128)} %param.20) | copy-start | bytes 110596
  11.0 26.0 %all-to-all-start = ((f32[128,3,1,8]{3,2,1,0:T(1,128)}), f32[128,3,1,8]{3,2,1,0:T(1,128)S(1)}, u32[]{:S(2)}, u32[]{:S(2)}) async-start(f32[128,3,1,8]{3,2,1,0:T(1,128)} %bitcast.27), calls=%async_computation | async-start | bytes 393216 | tf_op jit(solution)/shard_map/all_to_all | solution.py:27
  25.2 3.6 copy-start.10
  25.2 3.7 copy-start.11
  25.2 3.7 copy-start.17
  25.2 3.7 copy-start.18
  60.7 3.7 copy-start
  62.3 7.8 %collective-permute-start = (f32[2,2048]{1,0:T(2,128)S(1)}, f32[2,2048]{1,0:T(2,128)S(1)}, u32[]{:S(2)}, u32[]{:S(2)}) collective-permute-start(f32[2,2048]{1,0:T(2,128)S(1)} %copy.292), channel_id=1, source_target_pairs={{0,1},{1,2},{2,3},{3,4},{4,5},{5,6},{6,7},{7,8},{8,9},{9,10},{10,1... | collective-permute-start | bytes 49160 | tf_op jit(solution)/shard_map/while/body/eval_jaxpr/ppermute | solution.py:35
  67.8 2.0 copy-start.1
  69.8 1.2 copy-start.3
  85.0 5.2 %copy-start = (f32[2,2048]{0,1:T(8,128)S(1)}, f32[2,2048]{0,1:T(8,128)}, u32[]{:S(2)}) copy-start(f32[2,2048]{0,1:T(8,128)} %get-tuple-element.178) | copy-start | bytes 49156 | tf_op jit(solution)/shard_map/while
  86.7 9.3 %collective-permute-start = (f32[2,2048]{1,0:T(2,128)S(1)}, f32[2,2048]{1,0:T(2,128)S(1)}, u32[]{:S(2)}, u32[]{:S(2)}) collective-permute-start(f32[2,2048]{1,0:T(2,128)S(1)} %copy.292), channel_id=1, source_target_pairs={{0,1},{1,2},{2,3},{3,4},{4,5},{5,6},{6,7},{7,8},{8,9},{9,10},{10,1... | collective-permute-start | bytes 49160 | tf_op jit(solution)/shard_map/while/body/eval_jaxpr/ppermute | solution.py:35
  93.7 2.0 copy-start.1
  95.6 1.2 copy-start.3
  110.9 3.7 copy-start
  112.5 7.9 %collective-permute-start = (f32[2,2048]{1,0:T(2,128)S(1)}, f32[2,2048]{1,0:T(2,128)S(1)}, u32[]{:S(2)}, u32[]{:S(2)}) collective-permute-start(f32[2,2048]{1,0:T(2,128)S(1)} %copy.292), channel_id=1, source_target_pairs={{0,1},{1,2},{2,3},{3,4},{4,5},{5,6},{6,7},{7,8},{8,9},{9,10},{10,1... | collective-permute-start | bytes 49160 | tf_op jit(solution)/shard_map/while/body/eval_jaxpr/ppermute | solution.py:35
  118.0 2.0 copy-start.1
  120.0 1.2 copy-start.3
  135.2 5.3 %copy-start = (f32[2,2048]{0,1:T(8,128)S(1)}, f32[2,2048]{0,1:T(8,128)}, u32[]{:S(2)}) copy-start(f32[2,2048]{0,1:T(8,128)} %get-tuple-element.178) | copy-start | bytes 49156 | tf_op jit(solution)/shard_map/while
  136.9 9.4 %collective-permute-start = (f32[2,2048]{1,0:T(2,128)S(1)}, f32[2,2048]{1,0:T(2,128)S(1)}, u32[]{:S(2)}, u32[]{:S(2)}) collective-permute-start(f32[2,2048]{1,0:T(2,128)S(1)} %copy.292), channel_id=1, source_target_pairs={{0,1},{1,2},{2,3},{3,4},{4,5},{5,6},{6,7},{7,8},{8,9},{9,10},{10,1... | collective-permute-start | bytes 49160 | tf_op jit(solution)/shard_map/while/body/eval_jaxpr/ppermute | solution.py:35
  143.9 2.0 copy-start.1
  161.1 3.7 copy-start
  162.8 7.9 %collective-permute-start = (f32[2,2048]{1,0:T(2,128)S(1)}, f32[2,2048]{1,0:T(2,128)S(1)}, u32[]{:S(2)}, u32[]{:S(2)}) collective-permute-start(f32[2,2048]{1,0:T(2,128)S(1)} %copy.292), channel_id=1, source_target_pairs={{0,1},{1,2},{2,3},{3,4},{4,5},{5,6},{6,7},{7,8},{8,9},{9,10},{10,1... | collective-permute-start | bytes 49160 | tf_op jit(solution)/shard_map/while/body/eval_jaxpr/ppermute | solution.py:35
  168.3 2.0 copy-start.1
  170.3 1.2 copy-start.3
  185.5 5.0 %copy-start = (f32[2,2048]{0,1:T(8,128)S(1)}, f32[2,2048]{0,1:T(8,128)}, u32[]{:S(2)}) copy-start(f32[2,2048]{0,1:T(8,128)} %get-tuple-element.178) | copy-start | bytes 49156 | tf_op jit(solution)/shard_map/while
  187.1 9.1 %collective-permute-start = (f32[2,2048]{1,0:T(2,128)S(1)}, f32[2,2048]{1,0:T(2,128)S(1)}, u32[]{:S(2)}, u32[]{:S(2)}) collective-permute-start(f32[2,2048]{1,0:T(2,128)S(1)} %copy.292), channel_id=1, source_target_pairs={{0,1},{1,2},{2,3},{3,4},{4,5},{5,6},{6,7},{7,8},{8,9},{9,10},{10,1... | collective-permute-start | bytes 49160 | tf_op jit(solution)/shard_map/while/body/eval_jaxpr/ppermute | solution.py:35
  193.9 2.0 copy-start.1
  195.9 1.2 copy-start.3
  211.1 3.7 copy-start
  212.7 7.8 %collective-permute-start = (f32[2,2048]{1,0:T(2,128)S(1)}, f32[2,2048]{1,0:T(2,128)S(1)}, u32[]{:S(2)}, u32[]{:S(2)}) collective-permute-start(f32[2,2048]{1,0:T(2,128)S(1)} %copy.292), channel_id=1, source_target_pairs={{0,1},{1,2},{2,3},{3,4},{4,5},{5,6},{6,7},{7,8},{8,9},{9,10},{10,1... | collective-permute-start | bytes 49160 | tf_op jit(solution)/shard_map/while/body/eval_jaxpr/ppermute | solution.py:35
  218.3 2.0 copy-start.1
  220.2 1.2 copy-start.3
  235.5 4.3 %copy-start = (f32[2,2048]{0,1:T(8,128)S(1)}, f32[2,2048]{0,1:T(8,128)}, u32[]{:S(2)}) copy-start(f32[2,2048]{0,1:T(8,128)} %get-tuple-element.178) | copy-start | bytes 49156 | tf_op jit(solution)/shard_map/while
  237.1 8.4 %collective-permute-start = (f32[2,2048]{1,0:T(2,128)S(1)}, f32[2,2048]{1,0:T(2,128)S(1)}, u32[]{:S(2)}, u32[]{:S(2)}) collective-permute-start(f32[2,2048]{1,0:T(2,128)S(1)} %copy.292), channel_id=1, source_target_pairs={{0,1},{1,2},{2,3},{3,4},{4,5},{5,6},{6,7},{7,8},{8,9},{9,10},{10,1... | collective-permute-start | bytes 49160 | tf_op jit(solution)/shard_map/while/body/eval_jaxpr/ppermute | solution.py:35
  243.2 2.0 copy-start.1
  245.2 1.2 copy-start.3
  260.4 3.7 copy-start
  262.0 7.9 %collective-permute-start = (f32[2,2048]{1,0:T(2,128)S(1)}, f32[2,2048]{1,0:T(2,128)S(1)}, u32[]{:S(2)}, u32[]{:S(2)}) collective-permute-start(f32[2,2048]{1,0:T(2,128)S(1)} %copy.292), channel_id=1, source_target_pairs={{0,1},{1,2},{2,3},{3,4},{4,5},{5,6},{6,7},{7,8},{8,9},{9,10},{10,1... | collective-permute-start | bytes 49160 | tf_op jit(solution)/shard_map/while/body/eval_jaxpr/ppermute | solution.py:35
  267.6 2.0 copy-start.1
  284.8 5.2 %copy-start = (f32[2,2048]{0,1:T(8,128)S(1)}, f32[2,2048]{0,1:T(8,128)}, u32[]{:S(2)}) copy-start(f32[2,2048]{0,1:T(8,128)} %get-tuple-element.178) | copy-start | bytes 49156 | tf_op jit(solution)/shard_map/while
  286.4 9.4 %collective-permute-start = (f32[2,2048]{1,0:T(2,128)S(1)}, f32[2,2048]{1,0:T(2,128)S(1)}, u32[]{:S(2)}, u32[]{:S(2)}) collective-permute-start(f32[2,2048]{1,0:T(2,128)S(1)} %copy.292), channel_id=1, source_target_pairs={{0,1},{1,2},{2,3},{3,4},{4,5},{5,6},{6,7},{7,8},{8,9},{9,10},{10,1... | collective-permute-start | bytes 49160 | tf_op jit(solution)/shard_map/while/body/eval_jaxpr/ppermute | solution.py:35
  293.4 2.0 copy-start.1
  310.6 3.7 copy-start
  312.3 7.8 %collective-permute-start = (f32[2,2048]{1,0:T(2,128)S(1)}, f32[2,2048]{1,0:T(2,128)S(1)}, u32[]{:S(2)}, u32[]{:S(2)}) collective-permute-start(f32[2,2048]{1,0:T(2,128)S(1)} %copy.292), channel_id=1, source_target_pairs={{0,1},{1,2},{2,3},{3,4},{4,5},{5,6},{6,7},{7,8},{8,9},{9,10},{10,1... | collective-permute-start | bytes 49160 | tf_op jit(solution)/shard_map/while/body/eval_jaxpr/ppermute | solution.py:35
  317.8 2.0 copy-start.1
  319.8 1.2 copy-start.3
  335.0 5.3 %copy-start = (f32[2,2048]{0,1:T(8,128)S(1)}, f32[2,2048]{0,1:T(8,128)}, u32[]{:S(2)}) copy-start(f32[2,2048]{0,1:T(8,128)} %get-tuple-element.178) | copy-start | bytes 49156 | tf_op jit(solution)/shard_map/while
  336.6 9.4 %collective-permute-start = (f32[2,2048]{1,0:T(2,128)S(1)}, f32[2,2048]{1,0:T(2,128)S(1)}, u32[]{:S(2)}, u32[]{:S(2)}) collective-permute-start(f32[2,2048]{1,0:T(2,128)S(1)} %copy.292), channel_id=1, source_target_pairs={{0,1},{1,2},{2,3},{3,4},{4,5},{5,6},{6,7},{7,8},{8,9},{9,10},{10,1... | collective-permute-start | bytes 49160 | tf_op jit(solution)/shard_map/while/body/eval_jaxpr/ppermute | solution.py:35
  343.7 2.0 copy-start.1
  347.8 37.3 %copy-start.5 = (f32[48,64,128]{2,1,0:T(8,128)S(1)}, f32[48,64,128]{2,1,0:T(8,128)}, u32[]{:S(2)}) copy-start(f32[48,64,128]{2,1,0:T(8,128)} %copy-done.4) | copy-start | bytes 4718596
  374.7 20.2 %all-to-all-start.1 = ((f32[32,4,8]{2,1,0:T(4,128)}), f32[32,4,8]{2,1,0:T(4,128)S(1)}, u32[]{:S(2)}, u32[]{:S(2)}) async-start(f32[32,4,8]{2,1,0:T(4,128)} %constant_dynamic-update-slice_fusion), calls=%async_computation.1 | async-start | bytes 131072 | tf_op jit(solution)/shard_map/all_to_all | solution.py:143
  385.1 2.5 copy-start.7
  387.6 1.8 copy-start.6
  389.5 1.9 copy-start.8
  392.8 1.8 copy-start.2
  395.6 9.2 %all-to-all-start.2 = ((f32[4,1,256]{2,1,0:T(1,128)}), f32[4,1,256]{2,1,0:T(1,128)S(1)}, u32[]{:S(2)}, u32[]{:S(2)}) async-start(f32[4,1,256]{2,1,0:T(1,128)} %all_to_all.16), calls=%async_computation.2 | async-start | bytes 8192 | tf_op jit(solution)/shard_map/all_to_all | solution.py:153
  412.5 5.0 %copy-start.20 = (f32[128]{0:T(128)}, f32[128]{0:T(128)S(1)}, u32[]{:S(2)}) copy-start(f32[128]{0:T(128)S(1)} %slice.114) | copy-start | bytes 1540
  (5 other events, 5.7 us)
